TPU v7x, 512 devices: a whole 4x4x16 slice. The times are simulated.
512 devices in a mesh: dp: 128 (over z, x, y_lo), sub: 4 (over y_hi, core).
Axes of the slice: x: 4, y: 4 (y_hi: 2, y_lo: 2; y = y_hi * 2 + y_lo), z: 16, core: 2. Of those that a mesh axis runs over, the one named last changes fastest.
Arguments:
- queries: bfloat16 [16384, 4096], P('dp', 'sub'), may hold values from -1 to 1
- passages: bfloat16 [768, 4096], P('dp', 'sub'), may hold values from -1 to 1
- positive_bank: bfloat16 [2048, 4096], P('dp', 'sub'), may hold values from -1 to 1
- positive_ids: int32 [16384, 16], P('dp'), may hold values from -1 to 2047, as said below
- positive_counts: int32 [16384], P('dp'), may hold values from 1 to 16
Outputs:
- losses: float32 [16384], P('dp')
- query_grad: float32 [16384, 4096], P('dp', 'sub')
- passage_grad: float32 [768, 4096], P('dp', 'sub')
- bank_grad: float32 [2048, 4096], P('dp', 'sub')
Inputs may be any that keep to these rules, and one draw needn't show every extreme that they name: `positive_ids`: entries of row i before position positive_counts[i] are rows of positive_bank, the rest are -1. The valid entries of the 128 queries of one index of dp name rows held by any one index of dp at most 2 times in all (repeats counted), a bound that is reached. In each aligned block of 16 queries at most one query has more than one valid entry.
All inputs are finite; a program needn't handle non-finite values.
Results may differ from a plain program's by a relative error of at most 0.0019.
Values may be sent and summed in bfloat16 or wider, within the bound.
A program may use at most 64 MiB of HBM per device.

v0:
```python
import jax
import jax.numpy as jnp
from jax import lax
from jax.sharding import PartitionSpec as P


def softmax_terms(score_sums, pos_sums, counts):
    scores = score_sums * 50.0
    pos_scores = pos_sums * 50.0
    is_valid = jnp.arange(pos_scores.shape[1])[None, :] < counts[:, None]
    row_max = jnp.maximum(jnp.max(scores, 1), jnp.max(jnp.where(is_valid, pos_scores, -jnp.inf), 1))
    row_total = jnp.sum(jnp.exp(scores - row_max[:, None]), 1)
    row_total = row_total + jnp.sum(
        jnp.exp(jnp.where(is_valid, pos_scores - row_max[:, None], -jnp.inf)), 1
    )
    log_total = row_max + jnp.log(row_total)
    inv_count = 1.0 / counts.astype(jnp.float32)
    query_loss = log_total - jnp.sum(jnp.where(is_valid, pos_scores, 0.0), 1) * inv_count
    weights = jnp.exp(scores - log_total[:, None]).astype(jnp.bfloat16)
    coeffs = jnp.where(
        is_valid,
        jnp.exp(jnp.where(is_valid, pos_scores - log_total[:, None], -jnp.inf))
        - inv_count[:, None],
        0.0,
    )
    return (query_loss, weights, coeffs)


def body(queries, passages, positive_bank, positive_ids, positive_counts):
    peer_count = lax.axis_size("dp")
    query_count, col_width = queries.shape
    bank_rows = positive_bank.shape[0]
    capacity = bank_rows // 8
    max_pos = positive_ids.shape[1]
    slot_total = peer_count * capacity
    flat_ids = positive_ids.reshape(-1)
    is_live = (jnp.arange(max_pos)[None, :] < positive_counts[:, None]).reshape(-1)
    owner_dev = jnp.where(is_live, flat_ids // bank_rows, 0)
    onehot = ((owner_dev[:, None] == jnp.arange(peer_count)[None, :]) & is_live[:, None]).astype(
        jnp.int32
    )
    slot_rank = jnp.sum(jnp.cumsum(onehot, 0) * onehot, 1) - 1
    slot_of = jnp.where(is_live, owner_dev * capacity + slot_rank, slot_total)
    local_ids = jnp.where(is_live, flat_ids % bank_rows, -1)
    send_ids = jnp.full((slot_total + 1,), -1, jnp.int32).at[slot_of].set(local_ids)[:slot_total]
    slot_request = (
        jnp.zeros((slot_total + 1,), jnp.int32)
        .at[slot_of]
        .set(jnp.arange(flat_ids.shape[0], dtype=jnp.int32))[:slot_total]
    )
    slot_live = send_ids >= 0
    slot_query = slot_request // max_pos
    wanted = lax.all_to_all(
        send_ids.reshape(peer_count, capacity), "dp", split_axis=0, concat_axis=0, tiled=True
    ).reshape(-1)
    served = wanted >= 0
    picked = jnp.where(
        served[:, None],
        positive_bank[jnp.clip(wanted, 0, bank_rows - 1)],
        jnp.zeros((), jnp.bfloat16),
    )
    fetched = lax.all_to_all(
        picked.reshape(peer_count, capacity, col_width),
        "dp",
        split_axis=0,
        concat_axis=0,
        tiled=True,
    ).reshape(slot_total, col_width)
    query_slots = queries[slot_query]
    slot_scores = jnp.einsum("sd,sd->s", query_slots, fetched, preferred_element_type=jnp.float32)
    pos_part = jnp.concatenate([slot_scores, jnp.zeros((1,), jnp.float32)])[slot_of].reshape(
        query_count, max_pos
    )
    all_passages = lax.all_gather(passages, "dp", axis=0, tiled=True)
    score_part = lax.dot_general(
        queries, all_passages, (((1,), (1,)), ((), ())), preferred_element_type=jnp.float32
    )
    score_sums, pos_sums = lax.psum((score_part, pos_part), "sub")
    losses, weights, coeffs = softmax_terms(score_sums, pos_sums, positive_counts)
    slot_coeff = jnp.where(slot_live, coeffs.reshape(-1)[slot_request], 0.0)
    pos_grad = jax.ops.segment_sum(
        slot_coeff[:, None] * fetched.astype(jnp.float32), slot_query, query_count
    )
    query_grad = 50.0 * (
        jnp.dot(weights, all_passages, preferred_element_type=jnp.float32) + pos_grad
    )
    passage_grad = 50.0 * lax.psum_scatter(
        lax.dot_general(
            weights, queries, (((0,), (0,)), ((), ())), preferred_element_type=jnp.float32
        ),
        "dp",
        scatter_dimension=0,
        tiled=True,
    )
    grad_rows = (slot_coeff[:, None] * query_slots.astype(jnp.float32)).reshape(
        peer_count, capacity, col_width
    )
    bank_terms = lax.all_to_all(grad_rows, "dp", split_axis=0, concat_axis=0, tiled=True).reshape(
        slot_total, col_width
    )
    member = (
        jnp.where(served, wanted, bank_rows)[None, :] == jnp.arange(bank_rows)[:, None]
    ).astype(jnp.float32)
    bank_grad = 50.0 * jnp.dot(member, bank_terms, precision=lax.Precision.HIGHEST)
    return (losses, query_grad, passage_grad, bank_grad)


def solution(mesh):
    placed = (P("dp", "sub"), P("dp", "sub"), P("dp", "sub"), P("dp", None), P("dp"))
    return jax.shard_map(
        body,
        mesh=mesh,
        in_specs=placed,
        out_specs=(P("dp"), P("dp", "sub"), P("dp", "sub"), P("dp", "sub")),
        check_vma=False,
    )
```

profile of v0, /device:TPU:2, one launch (start us, length us, event | category | flops | bytes accessed | tf_op | source)
XLA Modules:
  0.0 1186.1 jit_solution(14348177609646131720)
XLA Ops:
  12.3 1.2 fusion.3
  13.5 8.0 scatter_custom_fusion.1
  21.7 34.5 %all_to_all.19 = s32[128,1,2]{2,1,0:T(1,128)S(1)} all-to-all(s32[128,1,2]{2,1,0:T(1,128)S(1)} %bitcast.24), channel_id=1, replica_groups=mesh['dp'=128,'sub'=4] {'dp'}, dimensions={0} | all-to-all | bytes 2048 | tf_op jit(solution)/shard_map/all_to_all | solution.py:53
  57.1 1.0 fusion.26
  58.3 1.2 gather_fusion.1
  59.7 1.4 broadcast_select_fusion
  61.0 6.6 all-to-all-start.1
  67.7 8.2 scatter_custom_fusion
  76.5 1.2 gather_fusion
  77.7 1.7 reshape.304
  79.3 18.1 %all-to-all-done.1 = bf16[128,2,1024]{2,1,0:T(2,128)(2,1)S(1)} async-done(((bf16[128,2,1024]{2,1,0:T(2,128)(2,1)}), bf16[128,2,1024]{2,1,0:T(2,128)(2,1)S(1)}, u32[]{:S(2)}, u32[]{:S(2)}) %all-to-all-start.1) | async-done | bytes 524320 | tf_op jit(solution)/shard_map/all_to_all | solution.py:62
  97.7 505.5 %all-gather.3.cloned.1.call-done = bf16[128,6,1024]{2,1,0:T(8,128)(2,1)} async-done(((bf16[1,6,1024]{2,1,0:T(8,128)(2,1)}), bf16[128,6,1024]{2,1,0:T(8,128)(2,1)}) %all-gather.3.cloned.1.call-update) | async-done | bytes 1572880 | tf_op jit(solution)/shard_map/all_gather | solution.py:74
  603.2 2.6 reshape.365
  605.8 1.4 fusion.27
  607.5 13.2 %gather_fusion.2 = f32[2048]{0:T(1024)S(1)} fusion(f32[257]{0:T(512)S(1)} %pad_maximum_fusion, s32[2048]{0:T(1024)S(1)} %broadcast_clamp_fusion), kind=kCustom, calls=%fused_computation.2 | custom fusion | bytes 24576 | tf_op jit(solution)/shard_map/gather | solution.py:71
  621.4 14.3 %psum.15 = f32[128,16]{1,0:T(8,128)S(1)} all-reduce(f32[128,16]{1,0:T(8,128)} %reshape.300), channel_id=1, replica_groups=mesh['dp'=128,'sub'=4] {'sub'}, use_global_device_ids=true, to_apply=%region_7.8 | all-reduce | flops 2048 | bytes 16384 | tf_op jit(solution)/shard_map/psum | solution.py:78
  635.9 26.8 %all-reduce.4.cloned.1.call-done = f32[128,768]{1,0:T(8,128)} async-done(((f32[128,768]{1,0:T(8,128)}), f32[128,768]{1,0:T(8,128)}) %all-reduce.4.cloned.1.call-update) | async-done | bytes 393232 | tf_op jit(solution)/shard_map/psum | solution.py:78
  662.7 1.1 multiply_reduce_fusion
  664.0 1.2 exponential_reduce_fusion
  666.5 0.9 reshape.301
  667.5 1.7 gather_fusion.3
  669.3 1.5 broadcast_multiply_fusion
  670.8 17.1 %all-to-all-start.2 = ((f32[128,2,1024]{2,1,0:T(2,128)}), f32[128,2,1024]{2,1,0:T(2,128)}, u32[]{:S(2)}, u32[]{:S(2)}) async-start(f32[128,2,1024]{2,1,0:T(2,128)} %broadcast_multiply_fusion), calls=%async_computation.2 | async-start | bytes 2097152 | tf_op jit(solution)/shard_map/all_to_all | solution.py:98
  688.0 2.3 fusion.24
  690.3 360.5 %fusion = f32[8,1024]{1,0:T(8,128)S(1)} fusion(f32[768,1024]{1,0:T(8,128)} %fusion.24), kind=kCustom, calls=%all-reduce-scatter | all-reduce-scatter fusion | flops 1048577 | bytes 3180544
  1050.8 12.1 %collective-permute-start.30 = (f32[8,1024]{1,0:T(8,128)S(1)}, f32[8,1024]{1,0:T(8,128)S(1)}, u32[]{:S(2)}, u32[]{:S(2)}) collective-permute-start(f32[8,1024]{1,0:T(8,128)S(1)} %fusion), channel_id=1, source_target_pairs={{0,124},{4,128},{8,132},{12,136},{16,140},{20,144},{24,148},{28,15... | collective-permute-start | bytes 98312
  1063.0 6.6 collective-permute-start.31
  1069.5 5.5 collective-permute-start.29
  1075.0 1.3 collective-permute-start.28
  1076.3 1.3 collective-permute-start.27
  1077.6 1.3 collective-permute-start.26
  1078.9 1.3 collective-permute-start.25
  1080.2 1.3 collective-permute-start.24
  1081.5 1.3 collective-permute-start.23
  1082.9 8.7 collective-permute-start.22
  1091.6 6.9 collective-permute-start.21
  1098.6 2.2 collective-permute-start.20
  1100.8 2.4 collective-permute-start.19
  1103.3 1.3 collective-permute-start.18
  1104.6 2.8 collective-permute-start.17
  1107.4 5.7 collective-permute-start.16
  1113.1 1.3 collective-permute-start.15
  1114.4 1.3 dynamic-slice.4
  1116.5 2.0 collective-permute-start.14
  1118.5 2.1 collective-permute-start.13
  1120.6 3.1 collective-permute-start.12
  1123.8 3.8 collective-permute-start.11
  1127.6 2.5 collective-permute-start.10
  1130.2 3.4 collective-permute-start.9
  1133.5 2.8 collective-permute-start.8
  1136.4 2.2 collective-permute-start.7
  1138.6 2.8 collective-permute-start.6
  1142.2 3.2 collective-permute-start.5
  1145.9 3.1 scatter_custom_fusion.2
  1149.1 2.5 collective-permute-start.4
  1151.6 2.5 collective-permute-start.3
  1154.0 4.3 collective-permute-start.2
  1158.4 3.1 collective-permute-start.1
  1161.5 3.6 collective-permute-start
  1165.1 0.8 broadcast_multiply_fusion.1
  1165.9 2.3 collective-permute-done
  1168.3 7.3 concatenate.4
  1176.3 1.9 reshape.303
  1178.2 1.1 convolution_multiply_fusion
  (161 shorter events, 12.1 us)
Async XLA Ops:
  7.2 69.3 %copy-start = (bf16[128,1024]{1,0:T(8,128)(2,1)S(1)}, bf16[128,1024]{1,0:T(8,128)(2,1)}, u32[]{:S(2)}) copy-start(bf16[128,1024]{1,0:T(8,128)(2,1)} %param.5) | copy-start | bytes 786436
  7.2 596.0 %all-gather.3.cloned.1.call-start = ((), (), s32[]{:S(2)}) async-start(), calls=%async_computation.4 | async-start | bytes 2113536 | tf_op jit(solution)/shard_map/all_gather | solution.py:74
  11.9 46.4 %copy-start.1 = (bf16[16,1024]{1,0:T(8,128)(2,1)S(1)}, bf16[16,1024]{1,0:T(8,128)(2,1)}, u32[]{:S(2)}) copy-start(bf16[16,1024]{1,0:T(8,128)(2,1)} %param.7) | copy-start | bytes 98308
  61.0 36.4 %all-to-all-start.1 = ((bf16[128,2,1024]{2,1,0:T(2,128)(2,1)}), bf16[128,2,1024]{2,1,0:T(2,128)(2,1)S(1)}, u32[]{:S(2)}, u32[]{:S(2)}) async-start(bf16[128,2,1024]{2,1,0:T(2,128)(2,1)} %broadcast_select_fusion), calls=%async_computation.1 | async-start | bytes 1048576 | tf_op jit(solution)/shard_map/all_to_all | solution.py:62
  67.6 595.1 %all-reduce.4.cloned.1.call-start = ((), (), s32[]{:S(2)}) async-start(), calls=%async_computation.3 | async-start | bytes 786432 | tf_op jit(solution)/shard_map/psum | solution.py:78
  607.5 28.3 %copy-start.34 = (s32[128]{0:T(128)S(1)}, s32[128]{0:T(128)}, u32[]{:S(2)}) copy-start(s32[128]{0:T(128)} %param.9) | copy-start | bytes 1540
  620.7 48.7 %copy-start.3 = (f32[128,2,1024]{2,1,0:T(2,128)S(1)}, f32[128,2,1024]{2,1,0:T(2,128)}, u32[]{:S(2)}) copy-start(f32[128,2,1024]{2,1,0:T(2,128)} %reshape.304) | copy-start | bytes 3145732
  670.8 505.4 %all-to-all-start.2 = ((f32[128,2,1024]{2,1,0:T(2,128)}), f32[128,2,1024]{2,1,0:T(2,128)}, u32[]{:S(2)}, u32[]{:S(2)}) async-start(f32[128,2,1024]{2,1,0:T(2,128)} %broadcast_multiply_fusion), calls=%async_computation.2 | async-start | bytes 2097152 | tf_op jit(solution)/shard_map/all_to_all | solution.py:98
  1050.8 28.1 %collective-permute-start.30 = (f32[8,1024]{1,0:T(8,128)S(1)}, f32[8,1024]{1,0:T(8,128)S(1)}, u32[]{:S(2)}, u32[]{:S(2)}) collective-permute-start(f32[8,1024]{1,0:T(8,128)S(1)} %fusion), channel_id=1, source_target_pairs={{0,124},{4,128},{8,132},{12,136},{16,140},{20,144},{24,148},{28,15... | collective-permute-start | bytes 98312
  1063.0 14.7 %collective-permute-start.31 = (f32[6,1024]{1,0:T(8,128)S(1)}, f32[6,1024]{1,0:T(8,128)S(1)}, u32[]{:S(2)}, u32[]{:S(2)}) collective-permute-start(f32[6,1024]{1,0:T(8,128)S(1)} %slice.26), channel_id=1, source_target_pairs={{0,128},{4,132},{8,136},{12,140},{16,144},{20,148},{24,152},{28,15... | collective-permute-start | bytes 73736
  1069.5 10.7 collective-permute-start.29
  1075.0 6.5 collective-permute-start.28
  1076.3 6.5 collective-permute-start.27
  1077.6 14.0 %collective-permute-start.26 = (f32[8,1024]{1,0:T(8,128)S(1)}, f32[8,1024]{1,0:T(8,128)S(1)}, u32[]{:S(2)}, u32[]{:S(2)}) collective-permute-start(f32[8,1024]{1,0:T(8,128)S(1)} %fusion), channel_id=1, source_target_pairs={{0,108},{4,112},{8,116},{12,120},{16,124},{20,128},{24,132},{28,13... | collective-permute-start | bytes 98312
  1078.9 19.6 %collective-permute-start.25 = (f32[8,1024]{1,0:T(8,128)S(1)}, f32[8,1024]{1,0:T(8,128)S(1)}, u32[]{:S(2)}, u32[]{:S(2)}) collective-permute-start(f32[8,1024]{1,0:T(8,128)S(1)} %fusion), channel_id=1, source_target_pairs={{0,104},{4,108},{8,112},{12,116},{16,120},{20,124},{24,128},{28,13... | collective-permute-start | bytes 98312
  1080.2 20.6 %collective-permute-start.24 = (f32[8,1024]{1,0:T(8,128)S(1)}, f32[8,1024]{1,0:T(8,128)S(1)}, u32[]{:S(2)}, u32[]{:S(2)}) collective-permute-start(f32[8,1024]{1,0:T(8,128)S(1)} %fusion), channel_id=1, source_target_pairs={{0,100},{4,104},{8,108},{12,112},{16,116},{20,120},{24,124},{28,12... | collective-permute-start | bytes 98312
  1081.5 21.7 %collective-permute-start.23 = (f32[8,1024]{1,0:T(8,128)S(1)}, f32[8,1024]{1,0:T(8,128)S(1)}, u32[]{:S(2)}, u32[]{:S(2)}) collective-permute-start(f32[8,1024]{1,0:T(8,128)S(1)} %fusion), channel_id=1, source_target_pairs={{0,96},{4,100},{8,104},{12,108},{16,112},{20,116},{24,120},{28,124... | collective-permute-start | bytes 98312
  1082.9 21.7 %collective-permute-start.22 = (f32[8,1024]{1,0:T(8,128)S(1)}, f32[8,1024]{1,0:T(8,128)S(1)}, u32[]{:S(2)}, u32[]{:S(2)}) collective-permute-start(f32[8,1024]{1,0:T(8,128)S(1)} %fusion), channel_id=1, source_target_pairs={{0,92},{4,96},{8,100},{12,104},{16,108},{20,112},{24,116},{28,120}... | collective-permute-start | bytes 98312
  1091.6 49.8 %copy-start.4 = (f32[8,1024]{1,0:T(8,128)}, f32[8,1024]{1,0:T(8,128)S(1)}, u32[]{:S(2)}) copy-start(f32[8,1024]{1,0:T(8,128)S(1)} %collective-permute-done.26) | copy-start | bytes 98308
  1091.6 15.7 %collective-permute-start.21 = (f32[8,1024]{1,0:T(8,128)S(1)}, f32[8,1024]{1,0:T(8,128)S(1)}, u32[]{:S(2)}, u32[]{:S(2)}) collective-permute-start(f32[8,1024]{1,0:T(8,128)S(1)} %fusion), channel_id=1, source_target_pairs={{0,88},{4,92},{8,96},{12,100},{16,104},{20,108},{24,112},{28,116},... | collective-permute-start | bytes 98312
  1098.6 42.9 %copy-start.6 = (f32[8,1024]{1,0:T(8,128)}, f32[8,1024]{1,0:T(8,128)S(1)}, u32[]{:S(2)}) copy-start(f32[8,1024]{1,0:T(8,128)S(1)} %collective-permute-done.25) | copy-start | bytes 98308
  1098.6 14.5 %collective-permute-start.20 = (f32[8,1024]{1,0:T(8,128)S(1)}, f32[8,1024]{1,0:T(8,128)S(1)}, u32[]{:S(2)}, u32[]{:S(2)}) collective-permute-start(f32[8,1024]{1,0:T(8,128)S(1)} %fusion), channel_id=1, source_target_pairs={{0,84},{4,88},{8,92},{12,96},{16,100},{20,104},{24,108},{28,112},{... | collective-permute-start | bytes 98312
  1100.8 40.6 %copy-start.8 = (f32[8,1024]{1,0:T(8,128)}, f32[8,1024]{1,0:T(8,128)S(1)}, u32[]{:S(2)}) copy-start(f32[8,1024]{1,0:T(8,128)S(1)} %collective-permute-done.24) | copy-start | bytes 98308
  1100.8 15.6 %collective-permute-start.19 = (f32[8,1024]{1,0:T(8,128)S(1)}, f32[8,1024]{1,0:T(8,128)S(1)}, u32[]{:S(2)}, u32[]{:S(2)}) collective-permute-start(f32[8,1024]{1,0:T(8,128)S(1)} %fusion), channel_id=1, source_target_pairs={{0,80},{4,84},{8,88},{12,92},{16,96},{20,100},{24,104},{28,108},{3... | collective-permute-start | bytes 98312
  1103.3 38.2 %copy-start.10 = (f32[8,1024]{1,0:T(8,128)}, f32[8,1024]{1,0:T(8,128)S(1)}, u32[]{:S(2)}) copy-start(f32[8,1024]{1,0:T(8,128)S(1)} %collective-permute-done.23) | copy-start | bytes 98308
  1103.3 15.2 %collective-permute-start.18 = (f32[8,1024]{1,0:T(8,128)S(1)}, f32[8,1024]{1,0:T(8,128)S(1)}, u32[]{:S(2)}, u32[]{:S(2)}) collective-permute-start(f32[8,1024]{1,0:T(8,128)S(1)} %fusion), channel_id=1, source_target_pairs={{0,76},{4,80},{8,84},{12,88},{16,92},{20,96},{24,100},{28,104},{32... | collective-permute-start | bytes 98312
  1104.6 36.9 %copy-start.12 = (f32[8,1024]{1,0:T(8,128)}, f32[8,1024]{1,0:T(8,128)S(1)}, u32[]{:S(2)}) copy-start(f32[8,1024]{1,0:T(8,128)S(1)} %collective-permute-done.22) | copy-start | bytes 98308
  1104.6 16.0 %collective-permute-start.17 = (f32[8,1024]{1,0:T(8,128)S(1)}, f32[8,1024]{1,0:T(8,128)S(1)}, u32[]{:S(2)}, u32[]{:S(2)}) collective-permute-start(f32[8,1024]{1,0:T(8,128)S(1)} %fusion), channel_id=1, source_target_pairs={{0,72},{4,76},{8,80},{12,84},{16,88},{20,92},{24,96},{28,100},{32,... | collective-permute-start | bytes 98312
  1107.4 34.1 %copy-start.14 = (f32[8,1024]{1,0:T(8,128)}, f32[8,1024]{1,0:T(8,128)S(1)}, u32[]{:S(2)}) copy-start(f32[8,1024]{1,0:T(8,128)S(1)} %collective-permute-done.21) | copy-start | bytes 98308
  1107.4 16.4 %collective-permute-start.16 = (f32[8,1024]{1,0:T(8,128)S(1)}, f32[8,1024]{1,0:T(8,128)S(1)}, u32[]{:S(2)}, u32[]{:S(2)}) collective-permute-start(f32[8,1024]{1,0:T(8,128)S(1)} %fusion), channel_id=1, source_target_pairs={{0,68},{4,72},{8,76},{12,80},{16,84},{20,88},{24,92},{28,96},{32,1... | collective-permute-start | bytes 98312
  1113.1 28.4 %copy-start.16 = (f32[8,1024]{1,0:T(8,128)}, f32[8,1024]{1,0:T(8,128)S(1)}, u32[]{:S(2)}) copy-start(f32[8,1024]{1,0:T(8,128)S(1)} %collective-permute-done.20) | copy-start | bytes 98308
  1113.1 14.5 %collective-permute-start.15 = (f32[8,1024]{1,0:T(8,128)S(1)}, f32[8,1024]{1,0:T(8,128)S(1)}, u32[]{:S(2)}, u32[]{:S(2)}) collective-permute-start(f32[8,1024]{1,0:T(8,128)S(1)} %fusion), channel_id=1, source_target_pairs={{0,64},{4,68},{8,72},{12,76},{16,80},{20,84},{24,88},{28,92},{32,9... | collective-permute-start | bytes 98312
  1116.5 25.0 %copy-start.18 = (f32[8,1024]{1,0:T(8,128)}, f32[8,1024]{1,0:T(8,128)S(1)}, u32[]{:S(2)}) copy-start(f32[8,1024]{1,0:T(8,128)S(1)} %collective-permute-done.19) | copy-start | bytes 98308
  1116.5 13.7 %collective-permute-start.14 = (f32[8,1024]{1,0:T(8,128)S(1)}, f32[8,1024]{1,0:T(8,128)S(1)}, u32[]{:S(2)}, u32[]{:S(2)}) collective-permute-start(f32[8,1024]{1,0:T(8,128)S(1)} %fusion), channel_id=1, source_target_pairs={{0,60},{4,64},{8,68},{12,72},{16,76},{20,80},{24,84},{28,88},{32,9... | collective-permute-start | bytes 98312
  1118.5 23.0 %copy-start.20 = (f32[8,1024]{1,0:T(8,128)}, f32[8,1024]{1,0:T(8,128)S(1)}, u32[]{:S(2)}) copy-start(f32[8,1024]{1,0:T(8,128)S(1)} %collective-permute-done.18) | copy-start | bytes 98308
  1118.5 15.0 %collective-permute-start.13 = (f32[8,1024]{1,0:T(8,128)S(1)}, f32[8,1024]{1,0:T(8,128)S(1)}, u32[]{:S(2)}, u32[]{:S(2)}) collective-permute-start(f32[8,1024]{1,0:T(8,128)S(1)} %fusion), channel_id=1, source_target_pairs={{0,56},{4,60},{8,64},{12,68},{16,72},{20,76},{24,80},{28,84},{32,8... | collective-permute-start | bytes 98312
  1120.6 15.8 %collective-permute-start.12 = (f32[8,1024]{1,0:T(8,128)S(1)}, f32[8,1024]{1,0:T(8,128)S(1)}, u32[]{:S(2)}, u32[]{:S(2)}) collective-permute-start(f32[8,1024]{1,0:T(8,128)S(1)} %fusion), channel_id=1, source_target_pairs={{0,52},{4,56},{8,60},{12,64},{16,68},{20,72},{24,76},{28,80},{32,8... | collective-permute-start | bytes 98312
  1123.8 14.8 %collective-permute-start.11 = (f32[8,1024]{1,0:T(8,128)S(1)}, f32[8,1024]{1,0:T(8,128)S(1)}, u32[]{:S(2)}, u32[]{:S(2)}) collective-permute-start(f32[8,1024]{1,0:T(8,128)S(1)} %fusion), channel_id=1, source_target_pairs={{0,48},{4,52},{8,56},{12,60},{16,64},{20,68},{24,72},{28,76},{32,8... | collective-permute-start | bytes 98312
  1127.6 13.8 %collective-permute-start.10 = (f32[8,1024]{1,0:T(8,128)S(1)}, f32[8,1024]{1,0:T(8,128)S(1)}, u32[]{:S(2)}, u32[]{:S(2)}) collective-permute-start(f32[8,1024]{1,0:T(8,128)S(1)} %fusion), channel_id=1, source_target_pairs={{0,44},{4,48},{8,52},{12,56},{16,60},{20,64},{24,68},{28,72},{32,7... | collective-permute-start | bytes 98312
  1130.2 18.9 %collective-permute-start.9 = (f32[8,1024]{1,0:T(8,128)S(1)}, f32[8,1024]{1,0:T(8,128)}, u32[]{:S(2)}, u32[]{:S(2)}) collective-permute-start(f32[8,1024]{1,0:T(8,128)S(1)} %fusion), channel_id=1, source_target_pairs={{0,40},{4,44},{8,48},{12,52},{16,56},{20,60},{24,64},{28,68},{32,7... | collective-permute-start | bytes 98312
  1133.5 18.0 %collective-permute-start.8 = (f32[8,1024]{1,0:T(8,128)S(1)}, f32[8,1024]{1,0:T(8,128)}, u32[]{:S(2)}, u32[]{:S(2)}) collective-permute-start(f32[8,1024]{1,0:T(8,128)S(1)} %fusion), channel_id=1, source_target_pairs={{0,36},{4,40},{8,44},{12,48},{16,52},{20,56},{24,60},{28,64},{32,6... | collective-permute-start | bytes 98312
  1136.4 17.6 %collective-permute-start.7 = (f32[8,1024]{1,0:T(8,128)S(1)}, f32[8,1024]{1,0:T(8,128)}, u32[]{:S(2)}, u32[]{:S(2)}) collective-permute-start(f32[8,1024]{1,0:T(8,128)S(1)} %fusion), channel_id=1, source_target_pairs={{0,32},{4,36},{8,40},{12,44},{16,48},{20,52},{24,56},{28,60},{32,6... | collective-permute-start | bytes 98312
  1138.6 19.8 %collective-permute-start.6 = (f32[8,1024]{1,0:T(8,128)S(1)}, f32[8,1024]{1,0:T(8,128)}, u32[]{:S(2)}, u32[]{:S(2)}) collective-permute-start(f32[8,1024]{1,0:T(8,128)S(1)} %fusion), channel_id=1, source_target_pairs={{0,28},{4,32},{8,36},{12,40},{16,44},{20,48},{24,52},{28,56},{32,6... | collective-permute-start | bytes 98312
  1142.2 19.3 %collective-permute-start.5 = (f32[8,1024]{1,0:T(8,128)S(1)}, f32[8,1024]{1,0:T(8,128)}, u32[]{:S(2)}, u32[]{:S(2)}) collective-permute-start(f32[8,1024]{1,0:T(8,128)S(1)} %fusion), channel_id=1, source_target_pairs={{0,24},{4,28},{8,32},{12,36},{16,40},{20,44},{24,48},{28,52},{32,5... | collective-permute-start | bytes 98312
  1145.8 22.4 %copy-start.5 = (f32[8,1024]{1,0:T(8,128)S(1)}, f32[8,1024]{1,0:T(8,128)}, u32[]{:S(2)}) copy-start(f32[8,1024]{1,0:T(8,128)} %copy-done.4) | copy-start | bytes 98308
  1145.8 22.4 %copy-start.7 = (f32[8,1024]{1,0:T(8,128)S(1)}, f32[8,1024]{1,0:T(8,128)}, u32[]{:S(2)}) copy-start(f32[8,1024]{1,0:T(8,128)} %copy-done.6) | copy-start | bytes 98308
  1145.8 22.4 %copy-start.9 = (f32[8,1024]{1,0:T(8,128)S(1)}, f32[8,1024]{1,0:T(8,128)}, u32[]{:S(2)}) copy-start(f32[8,1024]{1,0:T(8,128)} %copy-done.8) | copy-start | bytes 98308
  1145.8 22.4 %copy-start.11 = (f32[8,1024]{1,0:T(8,128)S(1)}, f32[8,1024]{1,0:T(8,128)}, u32[]{:S(2)}) copy-start(f32[8,1024]{1,0:T(8,128)} %copy-done.10) | copy-start | bytes 98308
  1145.8 22.4 %copy-start.13 = (f32[8,1024]{1,0:T(8,128)S(1)}, f32[8,1024]{1,0:T(8,128)}, u32[]{:S(2)}) copy-start(f32[8,1024]{1,0:T(8,128)} %copy-done.12) | copy-start | bytes 98308
  1145.8 22.4 %copy-start.15 = (f32[8,1024]{1,0:T(8,128)S(1)}, f32[8,1024]{1,0:T(8,128)}, u32[]{:S(2)}) copy-start(f32[8,1024]{1,0:T(8,128)} %copy-done.14) | copy-start | bytes 98308
  1145.8 22.4 %copy-start.17 = (f32[8,1024]{1,0:T(8,128)S(1)}, f32[8,1024]{1,0:T(8,128)}, u32[]{:S(2)}) copy-start(f32[8,1024]{1,0:T(8,128)} %copy-done.16) | copy-start | bytes 98308
  1145.8 22.4 %copy-start.19 = (f32[8,1024]{1,0:T(8,128)S(1)}, f32[8,1024]{1,0:T(8,128)}, u32[]{:S(2)}) copy-start(f32[8,1024]{1,0:T(8,128)} %copy-done.18) | copy-start | bytes 98308
  1145.8 22.4 %copy-start.21 = (f32[8,1024]{1,0:T(8,128)S(1)}, f32[8,1024]{1,0:T(8,128)}, u32[]{:S(2)}) copy-start(f32[8,1024]{1,0:T(8,128)} %copy-done.20) | copy-start | bytes 98308
  1145.9 22.4 %copy-start.23 = (f32[8,1024]{1,0:T(8,128)S(1)}, f32[8,1024]{1,0:T(8,128)}, u32[]{:S(2)}) copy-start(f32[8,1024]{1,0:T(8,128)} %copy-done.22) | copy-start | bytes 98308
  1145.9 22.4 %copy-start.25 = (f32[8,1024]{1,0:T(8,128)S(1)}, f32[8,1024]{1,0:T(8,128)}, u32[]{:S(2)}) copy-start(f32[8,1024]{1,0:T(8,128)} %copy-done.24) | copy-start | bytes 98308
  1145.9 22.4 %copy-start.27 = (f32[8,1024]{1,0:T(8,128)S(1)}, f32[8,1024]{1,0:T(8,128)}, u32[]{:S(2)}) copy-start(f32[8,1024]{1,0:T(8,128)} %copy-done.26) | copy-start | bytes 98308
  1145.9 22.4 %copy-start.29 = (f32[8,1024]{1,0:T(8,128)S(1)}, f32[8,1024]{1,0:T(8,128)}, u32[]{:S(2)}) copy-start(f32[8,1024]{1,0:T(8,128)} %copy-done.28) | copy-start | bytes 98308
  1145.9 22.4 %copy-start.31 = (f32[8,1024]{1,0:T(8,128)S(1)}, f32[8,1024]{1,0:T(8,128)}, u32[]{:S(2)}) copy-start(f32[8,1024]{1,0:T(8,128)} %copy-done.30) | copy-start | bytes 98308
  1145.9 22.4 %copy-start.33 = (f32[8,1024]{1,0:T(8,128)S(1)}, f32[8,1024]{1,0:T(8,128)}, u32[]{:S(2)}) copy-start(f32[8,1024]{1,0:T(8,128)} %copy-done.32) | copy-start | bytes 98308
  1149.1 16.9 %collective-permute-start.4 = (f32[8,1024]{1,0:T(8,128)S(1)}, f32[8,1024]{1,0:T(8,128)S(1)}, u32[]{:S(2)}, u32[]{:S(2)}) collective-permute-start(f32[8,1024]{1,0:T(8,128)S(1)} %fusion), channel_id=1, source_target_pairs={{0,20},{4,24},{8,28},{12,32},{16,36},{20,40},{24,44},{28,48},{32,5... | collective-permute-start | bytes 98312
  1151.6 14.4 %collective-permute-start.3 = (f32[8,1024]{1,0:T(8,128)S(1)}, f32[8,1024]{1,0:T(8,128)S(1)}, u32[]{:S(2)}, u32[]{:S(2)}) collective-permute-start(f32[8,1024]{1,0:T(8,128)S(1)} %fusion), channel_id=1, source_target_pairs={{0,16},{4,20},{8,24},{12,28},{16,32},{20,36},{24,40},{28,44},{32,4... | collective-permute-start | bytes 98312
  1154.0 11.9 %collective-permute-start.2 = (f32[8,1024]{1,0:T(8,128)S(1)}, f32[8,1024]{1,0:T(8,128)S(1)}, u32[]{:S(2)}, u32[]{:S(2)}) collective-permute-start(f32[8,1024]{1,0:T(8,128)S(1)} %fusion), channel_id=1, source_target_pairs={{0,12},{4,16},{8,20},{12,24},{16,28},{20,32},{24,36},{28,40},{32,4... | collective-permute-start | bytes 98312
  1158.4 7.5 collective-permute-start.1
  1161.5 6.7 collective-permute-start
  (7 other events, 78.4 us)
Sparse Core Ops, SparseCore 0:
  10.1 593.0 all-gather.2
  607.4 55.3 all-reduce.3
where the time goes:
time: 1190 us
  waiting for transfers between devices  554 us (47%)
  blocking collectives  409 us (34%)
  starting transfers between devices  131 us (11%)
  local copies, waits for them, and re-layouts  55.2 us (5%)
  other arithmetic  16.1 us (1%)
  between operations  15.9 us (1%)
    all_gather x1, waiting for transfers between devices, body(): all_passages = lax.all_gather(passages, 'dp', axis=0, tiled=True)  506 us
    unnamed x1, blocking collectives  361 us
    unnamed x32, starting transfers between devices  107 us
    all_to_all x1, blocking collectives, body(): lax.all_to_all(send_ids.reshape(peer_count, capacity), 'dp', split_axis=0...  34.5 us
    psum x1, waiting for transfers between devices, body(): score_sums, pos_sums = lax.psum((score_part, pos_part), 'sub')  26.8 us
  transfers between devices with their start and end apart: 36, of which 4 were waited for; matrix products, arithmetic and copies ran while one was open for 35% of the time, Pallas kernels for 0%

commit v1 on v0

--- a/solution.py
+++ b/solution.py
@@ -2,6 +2,7 @@
 import jax.numpy as jnp
 from jax import lax
 from jax.sharding import PartitionSpec as P
+from jax.lax import all_to_all, axis_size
 
 
 def softmax_terms(score_sums, pos_sums, counts):
@@ -71,7 +72,9 @@
     pos_part = jnp.concatenate([slot_scores, jnp.zeros((1,), jnp.float32)])[slot_of].reshape(
         query_count, max_pos
     )
-    all_passages = lax.all_gather(passages, "dp", axis=0, tiled=True)
+    all_passages = jnp.concatenate(
+        all_to_all(jnp.stack([passages] * axis_size("dp")), "dp", 0, 0), axis=0
+    )
     score_part = lax.dot_general(
         queries, all_passages, (((1,), (1,)), ((), ())), preferred_element_type=jnp.float32
     )

time: 1190 us -> 783 us (0.66)
  waiting for transfers between devices: 554 us -> 109 us
  blocking collectives: 409 us -> 445 us
    all_gather x1 -> x0, waiting for transfers between devices: 506 us -> none  [body(): all_passages = lax.all_gather(passages, 'dp', axis=0, tiled=True)]
    all_to_all x1, waiting for transfers between devices: 18.1 us -> 80.6 us  [body(): all_to_all(jnp.stack([passages] * axis_size('dp')), 'dp', 0, 0)]
    all_to_all x0 -> x1, blocking collectives: none -> 35.9 us  [body(): lax.all_to_all(picked.reshape(peer_count, capacity, col_width), 'dp', spl...]
  transfers between devices with their start and end apart: 36 -> 35, of which waited for: 4 -> 3; matrix products, arithmetic and copies ran while one was open for 35% -> 52% of each run, Pallas kernels for 0% -> 0%
where the time goes in v1:
time: 783 us; the launch traced here: 781 us
  blocking collectives  445 us (57%)
  starting transfers between devices  134 us (17%)
  waiting for transfers between devices  109 us (14%)
  local copies, waits for them, and re-layouts  56.6 us (7%)
  between operations  16 us (2%)
  other arithmetic  15.5 us (2%)
    unnamed x1, blocking collectives  361 us
    unnamed x32, starting transfers between devices  107 us
    all_to_all x1, waiting for transfers between devices, body(): all_to_all(jnp.stack([passages] * axis_size('dp')), 'dp', 0, 0)  80.6 us
    all_to_all x1, blocking collectives, body(): lax.all_to_all(picked.reshape(peer_count, capacity, col_width), 'dp', spl...  35.9 us
    all_to_all x1, blocking collectives, body(): lax.all_to_all(send_ids.reshape(peer_count, capacity), 'dp', split_axis=0...  34.4 us
    psum x1, waiting for transfers between devices, body(): score_sums, pos_sums = lax.psum((score_part, pos_part), 'sub')  25.6 us
    all_to_all x1, starting transfers between devices, body(): lax.all_to_all(grad_rows, 'dp', split_axis=0, concat_axis=0, tiled=True)  17.1 us
  transfers between devices with their start and end apart: 35, of which 3 were waited for; matrix products, arithmetic and copies ran while one was open for 52% of the time, Pallas kernels for 0%

profile of v1, /device:TPU:2, one launch (start us, length us, event | category | flops | bytes accessed | tf_op | source)
XLA Modules:
  0.0 780.9 jit_solution(15012784337791566148)
XLA Ops:
  11.6 1.2 fusion.3
  12.9 8.0 %scatter_custom_fusion.1 = s32[257]{0:T(512)S(1)} fusion(s32[2048]{0:T(1024)S(1)} %bitcast.22, s32[2048]{0:T(1024)S(1)} %get-tuple-element.15, s32[]{:T(128)} %constant.39.clone.1), kind=kCustom, calls=%fused_computation.79 | custom fusion | bytes 1032 | tf_op jit(solution)/shard_map/scatter | solution.py:46
  21.1 34.4 %all_to_all.24 = s32[128,1,2]{2,1,0:T(1,128)S(1)} all-to-all(s32[128,1,2]{2,1,0:T(1,128)S(1)} %bitcast.21), channel_id=1, replica_groups=mesh['dp'=128,'sub'=4] {'dp'}, dimensions={0} | all-to-all | bytes 2048 | tf_op jit(solution)/shard_map/all_to_all | solution.py:54
  56.0 1.0 fusion.26
  57.2 1.2 gather_fusion.1
  59.5 35.9 %all_to_all.25 = bf16[128,2,1024]{2,1,0:T(2,128)(2,1)S(1)} all-to-all(bf16[128,2,1024]{2,1,0:T(2,128)(2,1)S(1)} %broadcast_select_fusion), channel_id=1, replica_groups=mesh['dp'=128,'sub'=4] {'dp'}, dimensions={0} | all-to-all | bytes 1048576 | tf_op jit(solution)/shard_map/all_to_all | solution.py:63
  95.3 1.6 stack.2
  96.9 9.6 %all-to-all-start = ((bf16[128,6,1024]{2,1,0:T(8,128)(2,1)}), bf16[128,6,1024]{2,1,0:T(8,128)(2,1)}, u32[]{:S(2)}, u32[]{:S(2)}) async-start(bf16[128,6,1024]{2,1,0:T(8,128)(2,1)} %stack.2), calls=%async_computation | async-start | bytes 4194304 | tf_op jit(solution)/shard_map/all_to_all | solution.py:76
  106.8 8.0 %scatter_custom_fusion = s32[257]{0:T(512)S(1)} fusion(s32[2048]{0:T(1024)S(1)} %bitcast.23, s32[2048]{0:T(1024)S(1)} %iota.22, s32[]{:T(128)} %constant.32.clone.1), kind=kCustom, calls=%fused_computation.81 | custom fusion | bytes 1032 | tf_op jit(solution)/shard_map/scatter | solution.py:50
  115.4 1.2 gather_fusion
  116.5 1.7 reshape.310
  118.4 80.6 %all-to-all-done = bf16[128,6,1024]{2,1,0:T(8,128)(2,1)} async-done(((bf16[128,6,1024]{2,1,0:T(8,128)(2,1)}), bf16[128,6,1024]{2,1,0:T(8,128)(2,1)}, u32[]{:S(2)}, u32[]{:S(2)}) %all-to-all-start) | async-done | bytes 1572896 | tf_op jit(solution)/shard_map/all_to_all | solution.py:76
  199.0 2.6 reshape.300
  201.6 1.4 fusion.27
  203.3 13.2 %gather_fusion.2 = f32[2048]{0:T(1024)S(1)} fusion(f32[257]{0:T(512)S(1)} %pad_maximum_fusion, s32[2048]{0:T(1024)S(1)} %broadcast_clamp_fusion), kind=kCustom, calls=%fused_computation.2 | custom fusion | bytes 24576 | tf_op jit(solution)/shard_map/gather | solution.py:72
  217.2 14.2 %psum.15 = f32[128,16]{1,0:T(8,128)S(1)} all-reduce(f32[128,16]{1,0:T(8,128)} %reshape.306), channel_id=1, replica_groups=mesh['dp'=128,'sub'=4] {'sub'}, use_global_device_ids=true, to_apply=%region_7.8 | all-reduce | flops 2048 | bytes 16384 | tf_op jit(solution)/shard_map/psum | solution.py:81
  231.6 25.6 %all-reduce.4.cloned.1.call-done = f32[128,768]{1,0:T(8,128)} async-done(((f32[128,768]{1,0:T(8,128)}), f32[128,768]{1,0:T(8,128)}) %all-reduce.4.cloned.1.call-update) | async-done | bytes 393232 | tf_op jit(solution)/shard_map/psum | solution.py:81
  257.1 1.1 multiply_reduce_fusion
  258.5 1.2 exponential_reduce_fusion
  261.0 0.9 reshape.307
  261.9 1.7 gather_fusion.3
  263.8 1.5 broadcast_multiply_fusion
  265.2 17.1 %all-to-all-start.3 = ((f32[128,2,1024]{2,1,0:T(2,128)}), f32[128,2,1024]{2,1,0:T(2,128)}, u32[]{:S(2)}, u32[]{:S(2)}) async-start(f32[128,2,1024]{2,1,0:T(2,128)} %broadcast_multiply_fusion), calls=%async_computation.3 | async-start | bytes 2097152 | tf_op jit(solution)/shard_map/all_to_all | solution.py:101
  282.4 2.3 fusion.24
  284.7 360.5 %fusion = f32[8,1024]{1,0:T(8,128)S(1)} fusion(f32[768,1024]{1,0:T(8,128)} %fusion.24), kind=kCustom, calls=%all-reduce-scatter | all-reduce-scatter fusion | flops 1048577 | bytes 3180544
  645.2 12.1 %collective-permute-start.30 = (f32[8,1024]{1,0:T(8,128)S(1)}, f32[8,1024]{1,0:T(8,128)S(1)}, u32[]{:S(2)}, u32[]{:S(2)}) collective-permute-start(f32[8,1024]{1,0:T(8,128)S(1)} %fusion), channel_id=1, source_target_pairs={{0,124},{4,128},{8,132},{12,136},{16,140},{20,144},{24,148},{28,15... | collective-permute-start | bytes 98312
  657.4 6.6 collective-permute-start.31
  663.9 5.5 collective-permute-start.29
  669.4 1.3 collective-permute-start.28
  670.7 1.3 collective-permute-start.27
  672.0 1.3 collective-permute-start.26
  673.3 1.3 collective-permute-start.25
  674.7 1.3 collective-permute-start.24
  676.0 1.3 collective-permute-start.23
  677.3 8.8 %collective-permute-start.22 = (f32[8,1024]{1,0:T(8,128)S(1)}, f32[8,1024]{1,0:T(8,128)S(1)}, u32[]{:S(2)}, u32[]{:S(2)}) collective-permute-start(f32[8,1024]{1,0:T(8,128)S(1)} %fusion), channel_id=1, source_target_pairs={{0,92},{4,96},{8,100},{12,104},{16,108},{20,112},{24,116},{28,120}... | collective-permute-start | bytes 98312
  686.1 6.9 collective-permute-start.21
  693.0 2.2 collective-permute-start.20
  695.2 2.4 collective-permute-start.19
  697.7 1.3 collective-permute-start.18
  699.0 3.0 collective-permute-start.17
  702.0 5.4 collective-permute-start.16
  707.5 1.3 collective-permute-start.15
  708.8 1.3 dynamic-slice.4
  710.9 1.7 collective-permute-start.14
  712.6 2.0 collective-permute-start.13
  714.7 3.5 collective-permute-start.12
  718.2 3.8 collective-permute-start.11
  722.0 2.5 collective-permute-start.10
  724.6 3.4 collective-permute-start.9
  728.0 2.8 collective-permute-start.8
  730.8 2.2 collective-permute-start.7
  733.0 2.8 collective-permute-start.6
  736.6 3.2 collective-permute-start.5
  740.4 3.3 scatter_custom_fusion.2
  743.8 2.5 collective-permute-start.4
  746.3 2.4 collective-permute-start.3
  748.7 4.4 collective-permute-start.2
  753.1 3.1 collective-permute-start.1
  756.2 3.4 collective-permute-start
  759.6 0.8 broadcast_multiply_fusion.1
  760.5 2.5 collective-permute-done
  763.1 7.3 concatenate.4
  771.0 1.9 reshape.309
  773.0 1.1 convolution_multiply_fusion
  (170 shorter events, 12.1 us)
Async XLA Ops:
  7.2 108.2 %copy-start = (bf16[128,1024]{1,0:T(8,128)(2,1)S(1)}, bf16[128,1024]{1,0:T(8,128)(2,1)}, u32[]{:S(2)}) copy-start(bf16[128,1024]{1,0:T(8,128)(2,1)} %param.5) | copy-start | bytes 786436
  11.2 45.9 %copy-start.1 = (bf16[16,1024]{1,0:T(8,128)(2,1)S(1)}, bf16[16,1024]{1,0:T(8,128)(2,1)}, u32[]{:S(2)}) copy-start(bf16[16,1024]{1,0:T(8,128)(2,1)} %param.7) | copy-start | bytes 98308
  58.3 37.0 %copy-start.39 = (bf16[6,1024]{1,0:T(8,128)(2,1)S(1)}, bf16[6,1024]{1,0:T(8,128)(2,1)}, u32[]{:S(2)}) copy-start(bf16[6,1024]{1,0:T(8,128)(2,1)} %param.6) | copy-start | bytes 36868
  96.9 102.1 %all-to-all-start = ((bf16[128,6,1024]{2,1,0:T(8,128)(2,1)}), bf16[128,6,1024]{2,1,0:T(8,128)(2,1)}, u32[]{:S(2)}, u32[]{:S(2)}) async-start(bf16[128,6,1024]{2,1,0:T(8,128)(2,1)} %stack.2), calls=%async_computation | async-start | bytes 4194304 | tf_op jit(solution)/shard_map/all_to_all | solution.py:76
  106.5 150.6 %all-reduce.4.cloned.1.call-start = ((), (), s32[]{:S(2)}) async-start(), calls=%async_computation.4 | async-start | bytes 786432 | tf_op jit(solution)/shard_map/psum | solution.py:81
  203.3 28.1 %copy-start.38 = (s32[128]{0:T(128)S(1)}, s32[128]{0:T(128)}, u32[]{:S(2)}) copy-start(s32[128]{0:T(128)} %param.9) | copy-start | bytes 1540
  216.5 47.3 %copy-start.3 = (f32[128,2,1024]{2,1,0:T(2,128)S(1)}, f32[128,2,1024]{2,1,0:T(2,128)}, u32[]{:S(2)}) copy-start(f32[128,2,1024]{2,1,0:T(2,128)} %reshape.310) | copy-start | bytes 3145732
  265.2 505.8 %all-to-all-start.3 = ((f32[128,2,1024]{2,1,0:T(2,128)}), f32[128,2,1024]{2,1,0:T(2,128)}, u32[]{:S(2)}, u32[]{:S(2)}) async-start(f32[128,2,1024]{2,1,0:T(2,128)} %broadcast_multiply_fusion), calls=%async_computation.3 | async-start | bytes 2097152 | tf_op jit(solution)/shard_map/all_to_all | solution.py:101
  645.2 28.1 %collective-permute-start.30 = (f32[8,1024]{1,0:T(8,128)S(1)}, f32[8,1024]{1,0:T(8,128)S(1)}, u32[]{:S(2)}, u32[]{:S(2)}) collective-permute-start(f32[8,1024]{1,0:T(8,128)S(1)} %fusion), channel_id=1, source_target_pairs={{0,124},{4,128},{8,132},{12,136},{16,140},{20,144},{24,148},{28,15... | collective-permute-start | bytes 98312
  657.4 14.7 %collective-permute-start.31 = (f32[6,1024]{1,0:T(8,128)S(1)}, f32[6,1024]{1,0:T(8,128)S(1)}, u32[]{:S(2)}, u32[]{:S(2)}) collective-permute-start(f32[6,1024]{1,0:T(8,128)S(1)} %slice.26), channel_id=1, source_target_pairs={{0,128},{4,132},{8,136},{12,140},{16,144},{20,148},{24,152},{28,15... | collective-permute-start | bytes 73736
  663.9 10.7 %collective-permute-start.29 = (f32[8,1024]{1,0:T(8,128)S(1)}, f32[8,1024]{1,0:T(8,128)S(1)}, u32[]{:S(2)}, u32[]{:S(2)}) collective-permute-start(f32[8,1024]{1,0:T(8,128)S(1)} %fusion), channel_id=1, source_target_pairs={{0,120},{4,124},{8,128},{12,132},{16,136},{20,140},{24,144},{28,14... | collective-permute-start | bytes 98312
  669.4 6.5 collective-permute-start.28
  670.7 6.5 collective-permute-start.27
  672.0 14.0 %collective-permute-start.26 = (f32[8,1024]{1,0:T(8,128)S(1)}, f32[8,1024]{1,0:T(8,128)S(1)}, u32[]{:S(2)}, u32[]{:S(2)}) collective-permute-start(f32[8,1024]{1,0:T(8,128)S(1)} %fusion), channel_id=1, source_target_pairs={{0,108},{4,112},{8,116},{12,120},{16,124},{20,128},{24,132},{28,13... | collective-permute-start | bytes 98312
  673.3 19.6 %collective-permute-start.25 = (f32[8,1024]{1,0:T(8,128)S(1)}, f32[8,1024]{1,0:T(8,128)S(1)}, u32[]{:S(2)}, u32[]{:S(2)}) collective-permute-start(f32[8,1024]{1,0:T(8,128)S(1)} %fusion), channel_id=1, source_target_pairs={{0,104},{4,108},{8,112},{12,116},{16,120},{20,124},{24,128},{28,13... | collective-permute-start | bytes 98312
  674.7 20.6 %collective-permute-start.24 = (f32[8,1024]{1,0:T(8,128)S(1)}, f32[8,1024]{1,0:T(8,128)S(1)}, u32[]{:S(2)}, u32[]{:S(2)}) collective-permute-start(f32[8,1024]{1,0:T(8,128)S(1)} %fusion), channel_id=1, source_target_pairs={{0,100},{4,104},{8,108},{12,112},{16,116},{20,120},{24,124},{28,12... | collective-permute-start | bytes 98312
  676.0 21.7 %collective-permute-start.23 = (f32[8,1024]{1,0:T(8,128)S(1)}, f32[8,1024]{1,0:T(8,128)S(1)}, u32[]{:S(2)}, u32[]{:S(2)}) collective-permute-start(f32[8,1024]{1,0:T(8,128)S(1)} %fusion), channel_id=1, source_target_pairs={{0,96},{4,100},{8,104},{12,108},{16,112},{20,116},{24,120},{28,124... | collective-permute-start | bytes 98312
  677.3 21.7 %collective-permute-start.22 = (f32[8,1024]{1,0:T(8,128)S(1)}, f32[8,1024]{1,0:T(8,128)S(1)}, u32[]{:S(2)}, u32[]{:S(2)}) collective-permute-start(f32[8,1024]{1,0:T(8,128)S(1)} %fusion), channel_id=1, source_target_pairs={{0,92},{4,96},{8,100},{12,104},{16,108},{20,112},{24,116},{28,120}... | collective-permute-start | bytes 98312
  686.0 49.8 %copy-start.4 = (f32[8,1024]{1,0:T(8,128)}, f32[8,1024]{1,0:T(8,128)S(1)}, u32[]{:S(2)}) copy-start(f32[8,1024]{1,0:T(8,128)S(1)} %collective-permute-done.26) | copy-start | bytes 98308
  686.1 15.9 %collective-permute-start.21 = (f32[8,1024]{1,0:T(8,128)S(1)}, f32[8,1024]{1,0:T(8,128)S(1)}, u32[]{:S(2)}, u32[]{:S(2)}) collective-permute-start(f32[8,1024]{1,0:T(8,128)S(1)} %fusion), channel_id=1, source_target_pairs={{0,88},{4,92},{8,96},{12,100},{16,104},{20,108},{24,112},{28,116},... | collective-permute-start | bytes 98312
  693.0 42.9 %copy-start.6 = (f32[8,1024]{1,0:T(8,128)}, f32[8,1024]{1,0:T(8,128)S(1)}, u32[]{:S(2)}) copy-start(f32[8,1024]{1,0:T(8,128)S(1)} %collective-permute-done.25) | copy-start | bytes 98308
  693.0 14.5 %collective-permute-start.20 = (f32[8,1024]{1,0:T(8,128)S(1)}, f32[8,1024]{1,0:T(8,128)S(1)}, u32[]{:S(2)}, u32[]{:S(2)}) collective-permute-start(f32[8,1024]{1,0:T(8,128)S(1)} %fusion), channel_id=1, source_target_pairs={{0,84},{4,88},{8,92},{12,96},{16,100},{20,104},{24,108},{28,112},{... | collective-permute-start | bytes 98312
  695.2 40.6 %copy-start.8 = (f32[8,1024]{1,0:T(8,128)}, f32[8,1024]{1,0:T(8,128)S(1)}, u32[]{:S(2)}) copy-start(f32[8,1024]{1,0:T(8,128)S(1)} %collective-permute-done.24) | copy-start | bytes 98308
  695.2 15.6 %collective-permute-start.19 = (f32[8,1024]{1,0:T(8,128)S(1)}, f32[8,1024]{1,0:T(8,128)S(1)}, u32[]{:S(2)}, u32[]{:S(2)}) collective-permute-start(f32[8,1024]{1,0:T(8,128)S(1)} %fusion), channel_id=1, source_target_pairs={{0,80},{4,84},{8,88},{12,92},{16,96},{20,100},{24,104},{28,108},{3... | collective-permute-start | bytes 98312
  697.7 38.2 %copy-start.10 = (f32[8,1024]{1,0:T(8,128)}, f32[8,1024]{1,0:T(8,128)S(1)}, u32[]{:S(2)}) copy-start(f32[8,1024]{1,0:T(8,128)S(1)} %collective-permute-done.23) | copy-start | bytes 98308
  697.7 14.9 %collective-permute-start.18 = (f32[8,1024]{1,0:T(8,128)S(1)}, f32[8,1024]{1,0:T(8,128)S(1)}, u32[]{:S(2)}, u32[]{:S(2)}) collective-permute-start(f32[8,1024]{1,0:T(8,128)S(1)} %fusion), channel_id=1, source_target_pairs={{0,76},{4,80},{8,84},{12,88},{16,92},{20,96},{24,100},{28,104},{32... | collective-permute-start | bytes 98312
  699.0 36.8 %copy-start.12 = (f32[8,1024]{1,0:T(8,128)}, f32[8,1024]{1,0:T(8,128)S(1)}, u32[]{:S(2)}) copy-start(f32[8,1024]{1,0:T(8,128)S(1)} %collective-permute-done.22) | copy-start | bytes 98308
  699.0 15.6 %collective-permute-start.17 = (f32[8,1024]{1,0:T(8,128)S(1)}, f32[8,1024]{1,0:T(8,128)S(1)}, u32[]{:S(2)}, u32[]{:S(2)}) collective-permute-start(f32[8,1024]{1,0:T(8,128)S(1)} %fusion), channel_id=1, source_target_pairs={{0,72},{4,76},{8,80},{12,84},{16,88},{20,92},{24,96},{28,100},{32,... | collective-permute-start | bytes 98312
  702.0 33.9 %copy-start.14 = (f32[8,1024]{1,0:T(8,128)}, f32[8,1024]{1,0:T(8,128)S(1)}, u32[]{:S(2)}) copy-start(f32[8,1024]{1,0:T(8,128)S(1)} %collective-permute-done.21) | copy-start | bytes 98308
  702.0 16.2 %collective-permute-start.16 = (f32[8,1024]{1,0:T(8,128)S(1)}, f32[8,1024]{1,0:T(8,128)S(1)}, u32[]{:S(2)}, u32[]{:S(2)}) collective-permute-start(f32[8,1024]{1,0:T(8,128)S(1)} %fusion), channel_id=1, source_target_pairs={{0,68},{4,72},{8,76},{12,80},{16,84},{20,88},{24,92},{28,96},{32,1... | collective-permute-start | bytes 98312
  707.5 28.4 %copy-start.16 = (f32[8,1024]{1,0:T(8,128)}, f32[8,1024]{1,0:T(8,128)S(1)}, u32[]{:S(2)}) copy-start(f32[8,1024]{1,0:T(8,128)S(1)} %collective-permute-done.20) | copy-start | bytes 98308
  707.5 14.5 %collective-permute-start.15 = (f32[8,1024]{1,0:T(8,128)S(1)}, f32[8,1024]{1,0:T(8,128)S(1)}, u32[]{:S(2)}, u32[]{:S(2)}) collective-permute-start(f32[8,1024]{1,0:T(8,128)S(1)} %fusion), channel_id=1, source_target_pairs={{0,64},{4,68},{8,72},{12,76},{16,80},{20,84},{24,88},{28,92},{32,9... | collective-permute-start | bytes 98312
  710.9 25.0 %copy-start.18 = (f32[8,1024]{1,0:T(8,128)}, f32[8,1024]{1,0:T(8,128)S(1)}, u32[]{:S(2)}) copy-start(f32[8,1024]{1,0:T(8,128)S(1)} %collective-permute-done.19) | copy-start | bytes 98308
  710.9 13.7 %collective-permute-start.14 = (f32[8,1024]{1,0:T(8,128)S(1)}, f32[8,1024]{1,0:T(8,128)S(1)}, u32[]{:S(2)}, u32[]{:S(2)}) collective-permute-start(f32[8,1024]{1,0:T(8,128)S(1)} %fusion), channel_id=1, source_target_pairs={{0,60},{4,64},{8,68},{12,72},{16,76},{20,80},{24,84},{28,88},{32,9... | collective-permute-start | bytes 98312
  712.6 23.3 %copy-start.20 = (f32[8,1024]{1,0:T(8,128)}, f32[8,1024]{1,0:T(8,128)S(1)}, u32[]{:S(2)}) copy-start(f32[8,1024]{1,0:T(8,128)S(1)} %collective-permute-done.18) | copy-start | bytes 98308
  712.6 15.3 %collective-permute-start.13 = (f32[8,1024]{1,0:T(8,128)S(1)}, f32[8,1024]{1,0:T(8,128)S(1)}, u32[]{:S(2)}, u32[]{:S(2)}) collective-permute-start(f32[8,1024]{1,0:T(8,128)S(1)} %fusion), channel_id=1, source_target_pairs={{0,56},{4,60},{8,64},{12,68},{16,72},{20,76},{24,80},{28,84},{32,8... | collective-permute-start | bytes 98312
  714.7 16.1 %collective-permute-start.12 = (f32[8,1024]{1,0:T(8,128)S(1)}, f32[8,1024]{1,0:T(8,128)S(1)}, u32[]{:S(2)}, u32[]{:S(2)}) collective-permute-start(f32[8,1024]{1,0:T(8,128)S(1)} %fusion), channel_id=1, source_target_pairs={{0,52},{4,56},{8,60},{12,64},{16,68},{20,72},{24,76},{28,80},{32,8... | collective-permute-start | bytes 98312
  718.2 14.8 %collective-permute-start.11 = (f32[8,1024]{1,0:T(8,128)S(1)}, f32[8,1024]{1,0:T(8,128)S(1)}, u32[]{:S(2)}, u32[]{:S(2)}) collective-permute-start(f32[8,1024]{1,0:T(8,128)S(1)} %fusion), channel_id=1, source_target_pairs={{0,48},{4,52},{8,56},{12,60},{16,64},{20,68},{24,72},{28,76},{32,8... | collective-permute-start | bytes 98312
  722.0 13.8 %collective-permute-start.10 = (f32[8,1024]{1,0:T(8,128)S(1)}, f32[8,1024]{1,0:T(8,128)S(1)}, u32[]{:S(2)}, u32[]{:S(2)}) collective-permute-start(f32[8,1024]{1,0:T(8,128)S(1)} %fusion), channel_id=1, source_target_pairs={{0,44},{4,48},{8,52},{12,56},{16,60},{20,64},{24,68},{28,72},{32,7... | collective-permute-start | bytes 98312
  724.6 19.2 %collective-permute-start.9 = (f32[8,1024]{1,0:T(8,128)S(1)}, f32[8,1024]{1,0:T(8,128)}, u32[]{:S(2)}, u32[]{:S(2)}) collective-permute-start(f32[8,1024]{1,0:T(8,128)S(1)} %fusion), channel_id=1, source_target_pairs={{0,40},{4,44},{8,48},{12,52},{16,56},{20,60},{24,64},{28,68},{32,7... | collective-permute-start | bytes 98312
  728.0 18.3 %collective-permute-start.8 = (f32[8,1024]{1,0:T(8,128)S(1)}, f32[8,1024]{1,0:T(8,128)}, u32[]{:S(2)}, u32[]{:S(2)}) collective-permute-start(f32[8,1024]{1,0:T(8,128)S(1)} %fusion), channel_id=1, source_target_pairs={{0,36},{4,40},{8,44},{12,48},{16,52},{20,56},{24,60},{28,64},{32,6... | collective-permute-start | bytes 98312
  730.8 17.9 %collective-permute-start.7 = (f32[8,1024]{1,0:T(8,128)S(1)}, f32[8,1024]{1,0:T(8,128)}, u32[]{:S(2)}, u32[]{:S(2)}) collective-permute-start(f32[8,1024]{1,0:T(8,128)S(1)} %fusion), channel_id=1, source_target_pairs={{0,32},{4,36},{8,40},{12,44},{16,48},{20,52},{24,56},{28,60},{32,6... | collective-permute-start | bytes 98312
  733.0 20.1 %collective-permute-start.6 = (f32[8,1024]{1,0:T(8,128)S(1)}, f32[8,1024]{1,0:T(8,128)}, u32[]{:S(2)}, u32[]{:S(2)}) collective-permute-start(f32[8,1024]{1,0:T(8,128)S(1)} %fusion), channel_id=1, source_target_pairs={{0,28},{4,32},{8,36},{12,40},{16,44},{20,48},{24,52},{28,56},{32,6... | collective-permute-start | bytes 98312
  736.6 19.6 %collective-permute-start.5 = (f32[8,1024]{1,0:T(8,128)S(1)}, f32[8,1024]{1,0:T(8,128)}, u32[]{:S(2)}, u32[]{:S(2)}) collective-permute-start(f32[8,1024]{1,0:T(8,128)S(1)} %fusion), channel_id=1, source_target_pairs={{0,24},{4,28},{8,32},{12,36},{16,40},{20,44},{24,48},{28,52},{32,5... | collective-permute-start | bytes 98312
  740.2 22.7 %copy-start.5 = (f32[8,1024]{1,0:T(8,128)S(1)}, f32[8,1024]{1,0:T(8,128)}, u32[]{:S(2)}) copy-start(f32[8,1024]{1,0:T(8,128)} %copy-done.4) | copy-start | bytes 98308
  740.2 22.7 %copy-start.7 = (f32[8,1024]{1,0:T(8,128)S(1)}, f32[8,1024]{1,0:T(8,128)}, u32[]{:S(2)}) copy-start(f32[8,1024]{1,0:T(8,128)} %copy-done.6) | copy-start | bytes 98308
  740.2 22.7 %copy-start.9 = (f32[8,1024]{1,0:T(8,128)S(1)}, f32[8,1024]{1,0:T(8,128)}, u32[]{:S(2)}) copy-start(f32[8,1024]{1,0:T(8,128)} %copy-done.8) | copy-start | bytes 98308
  740.3 22.7 %copy-start.11 = (f32[8,1024]{1,0:T(8,128)S(1)}, f32[8,1024]{1,0:T(8,128)}, u32[]{:S(2)}) copy-start(f32[8,1024]{1,0:T(8,128)} %copy-done.10) | copy-start | bytes 98308
  740.3 22.7 %copy-start.13 = (f32[8,1024]{1,0:T(8,128)S(1)}, f32[8,1024]{1,0:T(8,128)}, u32[]{:S(2)}) copy-start(f32[8,1024]{1,0:T(8,128)} %copy-done.12) | copy-start | bytes 98308
  740.3 22.7 %copy-start.15 = (f32[8,1024]{1,0:T(8,128)S(1)}, f32[8,1024]{1,0:T(8,128)}, u32[]{:S(2)}) copy-start(f32[8,1024]{1,0:T(8,128)} %copy-done.14) | copy-start | bytes 98308
  740.3 22.7 %copy-start.17 = (f32[8,1024]{1,0:T(8,128)S(1)}, f32[8,1024]{1,0:T(8,128)}, u32[]{:S(2)}) copy-start(f32[8,1024]{1,0:T(8,128)} %copy-done.16) | copy-start | bytes 98308
  740.3 22.7 %copy-start.19 = (f32[8,1024]{1,0:T(8,128)S(1)}, f32[8,1024]{1,0:T(8,128)}, u32[]{:S(2)}) copy-start(f32[8,1024]{1,0:T(8,128)} %copy-done.18) | copy-start | bytes 98308
  740.3 22.7 %copy-start.21 = (f32[8,1024]{1,0:T(8,128)S(1)}, f32[8,1024]{1,0:T(8,128)}, u32[]{:S(2)}) copy-start(f32[8,1024]{1,0:T(8,128)} %copy-done.20) | copy-start | bytes 98308
  740.3 22.7 %copy-start.23 = (f32[8,1024]{1,0:T(8,128)S(1)}, f32[8,1024]{1,0:T(8,128)}, u32[]{:S(2)}) copy-start(f32[8,1024]{1,0:T(8,128)} %copy-done.22) | copy-start | bytes 98308
  740.3 22.7 %copy-start.25 = (f32[8,1024]{1,0:T(8,128)S(1)}, f32[8,1024]{1,0:T(8,128)}, u32[]{:S(2)}) copy-start(f32[8,1024]{1,0:T(8,128)} %copy-done.24) | copy-start | bytes 98308
  740.3 22.7 %copy-start.27 = (f32[8,1024]{1,0:T(8,128)S(1)}, f32[8,1024]{1,0:T(8,128)}, u32[]{:S(2)}) copy-start(f32[8,1024]{1,0:T(8,128)} %copy-done.26) | copy-start | bytes 98308
  740.4 22.7 %copy-start.29 = (f32[8,1024]{1,0:T(8,128)S(1)}, f32[8,1024]{1,0:T(8,128)}, u32[]{:S(2)}) copy-start(f32[8,1024]{1,0:T(8,128)} %copy-done.28) | copy-start | bytes 98308
  740.4 22.7 %copy-start.31 = (f32[8,1024]{1,0:T(8,128)S(1)}, f32[8,1024]{1,0:T(8,128)}, u32[]{:S(2)}) copy-start(f32[8,1024]{1,0:T(8,128)} %copy-done.30) | copy-start | bytes 98308
  740.4 22.7 %copy-start.33 = (f32[8,1024]{1,0:T(8,128)S(1)}, f32[8,1024]{1,0:T(8,128)}, u32[]{:S(2)}) copy-start(f32[8,1024]{1,0:T(8,128)} %copy-done.32) | copy-start | bytes 98308
  743.8 16.7 %collective-permute-start.4 = (f32[8,1024]{1,0:T(8,128)S(1)}, f32[8,1024]{1,0:T(8,128)S(1)}, u32[]{:S(2)}, u32[]{:S(2)}) collective-permute-start(f32[8,1024]{1,0:T(8,128)S(1)} %fusion), channel_id=1, source_target_pairs={{0,20},{4,24},{8,28},{12,32},{16,36},{20,40},{24,44},{28,48},{32,5... | collective-permute-start | bytes 98312
  746.3 14.2 %collective-permute-start.3 = (f32[8,1024]{1,0:T(8,128)S(1)}, f32[8,1024]{1,0:T(8,128)S(1)}, u32[]{:S(2)}, u32[]{:S(2)}) collective-permute-start(f32[8,1024]{1,0:T(8,128)S(1)} %fusion), channel_id=1, source_target_pairs={{0,16},{4,20},{8,24},{12,28},{16,32},{20,36},{24,40},{28,44},{32,4... | collective-permute-start | bytes 98312
  748.7 11.8 %collective-permute-start.2 = (f32[8,1024]{1,0:T(8,128)S(1)}, f32[8,1024]{1,0:T(8,128)S(1)}, u32[]{:S(2)}, u32[]{:S(2)}) collective-permute-start(f32[8,1024]{1,0:T(8,128)S(1)} %fusion), channel_id=1, source_target_pairs={{0,12},{4,16},{8,20},{12,24},{16,28},{20,32},{24,36},{28,40},{32,4... | collective-permute-start | bytes 98312
  753.1 7.3 collective-permute-start.1
  756.2 6.7 collective-permute-start
  (11 other events, 151.2 us)
Sparse Core Ops, SparseCore 0:
  203.1 53.9 all-reduce.3
